TPU v7x, 32 devices: a whole 2x2x4 slice. The times are simulated.
32 devices in a mesh: group: 2 (over x), dev: 16 (over z, y, core).
Axes of the slice: x: 2, y: 2, z: 4, core: 2. Of those that a mesh axis runs over, the one named last changes fastest.
Arguments:
- residual: bfloat16 [32, 8192], P(('group', 'dev')), parts along dimension 0, may hold values from -36 to 36
- queries: bfloat16 [32, 8192], P(('group', 'dev')), parts along dimension 0, may hold values from -8 to 8
- fresh_keys: bfloat16 [32, 512], P(('group', 'dev')), parts along dimension 0, may hold values from -6 to 6
- fresh_values: bfloat16 [32, 512], P(('group', 'dev')), parts along dimension 0, may hold values from -15 to 15
- key_cache: bfloat16 [32, 320, 512], P(('group', 'dev')), parts along dimension 0, may hold values from -8 to 8
- value_cache: bfloat16 [32, 320, 512], P(('group', 'dev')), parts along dimension 0, may hold values from -15 to 15
- lengths: int32 [32], P(('group', 'dev')), parts along dimension 0, may hold values from 40 to 320, as said below
- keep_inputs: int32 [32, 64], P('group'), parts along dimension 0, may hold values 0 or 1
- keep_hidden: int32 [32, 216], P('group'), parts along dimension 0, may hold values 0 or 1
- norm_gain: float32 [8192], replicated, may hold values from 0.1 to 1.9
- out_weight: bfloat16 [8192, 8192], P('dev'), may hold values from -0.0625 to 0.0625
- gate_weight: bfloat16 [27648, 8192], P('dev'), may hold values from -0.0625 to 0.0625
- up_weight: bfloat16 [27648, 8192], P('dev'), may hold values from -0.0625 to 0.0625
- down_weight: bfloat16 [27648, 8192], P('dev'), may hold values from -0.0390625 to 0.0390625
Outputs:
- post_attention: bfloat16 [32, 8192], P(('group', 'dev')), parts along dimension 0
- layer_out: bfloat16 [32, 8192], P(('group', 'dev')), parts along dimension 0
There are 2 independent parts, one for each index of `group`. A program takes and returns all parts, laid end to end along the dimension named above; an argument that names none is the same for every part. Nothing has to cross between parts.
Inputs may be any that keep to these rules, and one draw needn't show every extreme that they name: `lengths`: some row has exactly 320 live slots.
All inputs are finite; a program needn't handle non-finite values.
Results may differ from a plain program's by a relative error of at most 0.0055.
Values may be sent and summed in bfloat16 or wider, within the bound.
A program may use at most 192 MiB of HBM per device.

v0:
```python
import math

import jax
import jax.numpy as jnp
from jax import lax
from jax.sharding import PartitionSpec as P

H = 64
KVH = 4
BLK = 128


def attend_rows(queries, fresh_keys, fresh_values, key_cache, value_cache, lengths):
    row_count, cache_span, kv_width = key_cache.shape
    head_dim = kv_width // KVH
    group_size = H // KVH
    grouped = queries.reshape(row_count, KVH, group_size, head_dim)
    key_rows = key_cache.reshape(row_count, cache_span, KVH, head_dim)
    value_rows = value_cache.reshape(row_count, cache_span, KVH, head_dim)
    score_scale = 1.0 / math.sqrt(head_dim)
    cached_scores = (
        jnp.einsum("rkgd,rlkd->rkgl", grouped, key_rows, preferred_element_type=jnp.float32)
        * score_scale
    )
    alive_mask = (jnp.arange(cache_span)[None, :] < lengths[:, None])[:, None, None, :]
    cached_scores = jnp.where(alive_mask, cached_scores, -1e30)
    fresh_scores = (
        jnp.einsum(
            "rkgd,rkd->rkg",
            grouped,
            fresh_keys.reshape(row_count, KVH, head_dim),
            preferred_element_type=jnp.float32,
        )
        * score_scale
    )
    highest = jnp.maximum(jnp.max(cached_scores, axis=-1), fresh_scores)
    cached_weights = jnp.where(alive_mask, jnp.exp(cached_scores - highest[..., None]), 0.0)
    fresh_weights = jnp.exp(fresh_scores - highest)
    totals = jnp.sum(cached_weights, axis=-1) + fresh_weights
    cached_probs = (cached_weights / totals[..., None]).astype(jnp.bfloat16)
    fresh_probs = (fresh_weights / totals).astype(jnp.bfloat16)
    blended = jnp.einsum(
        "rkgl,rlkd->rkgd", cached_probs, value_rows, preferred_element_type=jnp.float32
    )
    new_values = fresh_values.reshape(row_count, KVH, 1, head_dim).astype(jnp.float32)
    blended = blended + fresh_probs.astype(jnp.float32)[..., None] * new_values
    return blended.reshape(row_count, H * head_dim).astype(jnp.bfloat16)


def normalize(stream, norm_gain, keep_mask):
    row_count = stream.shape[0]
    squares = jnp.mean(stream * stream, axis=-1, keepdims=True)
    scaled = stream * lax.rsqrt(squares + 1e-05) * norm_gain
    blocked = scaled.reshape(row_count, keep_mask.shape[1], -1) * keep_mask[:, :, None].astype(
        jnp.float32
    )
    return blocked.reshape(row_count, -1).astype(jnp.bfloat16)


def shards(
    residual,
    queries,
    fresh_keys,
    fresh_values,
    key_cache,
    value_cache,
    lengths,
    keep_inputs,
    keep_hidden,
    norm_gain,
    out_weight,
    gate_weight,
    up_weight,
    down_weight,
):
    local_rows = residual.shape[0]
    first_row = lax.axis_index("dev") * local_rows
    attended = attend_rows(queries, fresh_keys, fresh_values, key_cache, value_cache, lengths)
    by_feature = lax.all_to_all(attended, "dev", split_axis=1, concat_axis=0, tiled=True)
    hidden_count = gate_weight.shape[0]
    unit_ids = lax.axis_index("dev") * hidden_count + jnp.arange(hidden_count)
    block_count = keep_hidden.shape[1]
    selector = (unit_ids[None, :] // BLK == jnp.arange(block_count)[:, None]).astype(jnp.float32)
    unit_keep = jnp.dot(keep_hidden.astype(jnp.float32), selector)
    contract = (((1,), (1,)), ((), ()))
    picked = by_feature
    summed = lax.psum_scatter(
        jnp.dot(picked, out_weight, preferred_element_type=jnp.float32),
        "dev",
        scatter_dimension=0,
        tiled=True,
    )
    post_attention = (residual.astype(jnp.float32) + summed).astype(jnp.bfloat16)
    keep_local = lax.dynamic_slice_in_dim(keep_inputs, first_row, local_rows, 0)
    ffn_input = normalize(post_attention.astype(jnp.float32), norm_gain, keep_local)
    inputs = lax.all_gather(ffn_input, "dev", axis=0, tiled=True)
    gate_proj = lax.dot_general(inputs, gate_weight, contract, preferred_element_type=jnp.float32)
    up_proj = lax.dot_general(inputs, up_weight, contract, preferred_element_type=jnp.float32)
    activated = (jax.nn.silu(gate_proj) * up_proj * unit_keep).astype(jnp.bfloat16)
    picked = activated
    ffn_out = lax.psum_scatter(
        jnp.dot(picked, down_weight, preferred_element_type=jnp.float32),
        "dev",
        scatter_dimension=0,
        tiled=True,
    )
    layer_out = (post_attention.astype(jnp.float32) + ffn_out).astype(jnp.bfloat16)
    return (post_attention, layer_out)


def solution(mesh):
    in_specs = (
        P(("group", "dev"), None),
        P(("group", "dev"), None),
        P(("group", "dev"), None),
        P(("group", "dev"), None),
        P(("group", "dev"), None, None),
        P(("group", "dev"), None, None),
        P(("group", "dev")),
        P("group", None),
        P("group", None),
        P(),
        P("dev", None),
        P("dev", None),
        P("dev", None),
        P("dev", None),
    )
    out_specs = (P(("group", "dev"), None), P(("group", "dev"), None))
    return jax.shard_map(shards, mesh=mesh, in_specs=in_specs, out_specs=out_specs, check_vma=False)
```

profile of v0, /device:TPU:0, one launch (start us, length us, event | category | flops | bytes accessed | tf_op | source)
XLA Modules:
  0.0 279.9 jit_solution(138177089906669645)
XLA Ops:
  7.8 0.7 convert_element_type.90
  8.5 1.1 reshape.186
  9.7 0.8 fusion.35
  10.5 0.3 fusion.42
  10.8 0.2 fusion.20
  11.0 1.1 reshape.188
  12.1 0.2 fusion.4
  12.3 0.5 broadcast.82
  12.8 0.7 reduce.6
  13.6 0.6 reshape.198
  14.2 7.4 %all-to-all-start = ((bf16[16,2,256]{2,1,0:T(2,128)(2,1)}), bf16[16,2,256]{2,1,0:T(2,128)(2,1)S(1)}, u32[]{:S(2)}, u32[]{:S(2)}) async-start(bf16[16,2,256]{2,1,0:T(2,128)(2,1)} %reshape.198), calls=%async_computation | async-start | bytes 32768 | tf_op jit(solution)/shard_map/all_to_all | solution.py:79
  21.7 6.4 %all-to-all-done = bf16[16,2,256]{2,1,0:T(2,128)(2,1)S(1)} async-done(((bf16[16,2,256]{2,1,0:T(2,128)(2,1)}), bf16[16,2,256]{2,1,0:T(2,128)(2,1)S(1)}, u32[]{:S(2)}, u32[]{:S(2)}) %all-to-all-start) | async-done | bytes 16416 | tf_op jit(solution)/shard_map/all_to_all | solution.py:79
  28.1 5.4 %fusion.28 = f32[16,8192]{1,0:T(8,128)} fusion(bf16[512,8192]{1,0:T(8,128)(2,1)} %param.24, bf16[1,16,512]{2,0,1:T(2,128)(2,1)S(1)} %bitcast.37), kind=kOutput, calls=%fused_computation.37 | convolution fusion | flops 134217728 | bytes 8929280 | tf_op jit(solution)/shard_map/dot_general | solution.py:88
  33.6 0.7 convert_bitcast_fusion.1
  34.3 1.3 dynamic-slice
  35.6 1.1 convolution_bitcast_fusion
  36.7 84.3 %all-reduce.5.cloned.1.call-done = f32[16,8192]{1,0:T(8,128)} async-done(((f32[16,8192]{1,0:T(8,128)}), f32[16,8192]{1,0:T(8,128)}) %all-reduce.5.cloned.1.call-update) | async-done | bytes 524304
  121.0 2.3 multiply_reduce_fusion
  124.1 0.8 convert_bitcast_fusion
  124.9 22.3 %all-gather = bf16[16,1,8192]{2,1,0:T(2,128)(2,1)S(1)} all-gather(bf16[1,1,8192]{2,1,0:T(2,128)(2,1)S(1)} %convert_bitcast_fusion), channel_id=1, replica_groups=mesh['group'=2,'dev'=16] {'dev'}, dimensions={0}, use_global_device_ids=true | all-gather | bytes 278528 | tf_op jit(solution)/shard_map/all_gather | solution.py:96
  147.2 12.8 %fusion.10 = f32[16,1728]{1,0:T(8,128)S(1)} fusion(bf16[1728,8192]{1,0:T(8,128)(2,1)} %param.25, bf16[16,1,8192]{2,1,0:T(2,128)(2,1)S(1)} %all-gather), kind=kOutput, calls=%fused_computation.14 | convolution fusion | flops 452984832 | bytes 28684288 | tf_op jit(solution)/shard_map/dot_general | solution.py:97
  160.0 23.3 %fusion.2 = f32[16,8192]{1,0:T(8,128)} fusion(bf16[1728,8192]{1,0:T(8,128)(2,1)} %param.27, f32[16,1728]{1,0:T(8,128)S(1)} %convolution_bitcast_fusion, bf16[1728,8192]{1,0:T(8,128)(2,1)} %param.26, f32[16,1728]{1,0:T(8,128)S(1)} %fusion.10, bf16[16,1,8192]{2,1,0:T(2,128)(2,1)S(1)} %all-gather), kind=kOutput, calls=%fused_computation.4 | convolution fusion | flops 906163200 | bytes 57630720 | tf_op jit(solution)/shard_map/dot_general | solution.py:102
  183.3 87.5 %all-reduce.7.cloned.1.call-done = f32[16,8192]{1,0:T(8,128)} async-done(((f32[16,8192]{1,0:T(8,128)}), f32[16,8192]{1,0:T(8,128)}) %all-reduce.7.cloned.1.call-update) | async-done | bytes 524304
  270.8 2.3 fusion.26
  (18 shorter events, 0.4 us)
Async XLA Ops:
  7.2 2.4 copy-start
  14.2 13.9 %all-to-all-start = ((bf16[16,2,256]{2,1,0:T(2,128)(2,1)}), bf16[16,2,256]{2,1,0:T(2,128)(2,1)S(1)}, u32[]{:S(2)}, u32[]{:S(2)}) async-start(bf16[16,2,256]{2,1,0:T(2,128)(2,1)} %reshape.198), calls=%async_computation | async-start | bytes 32768 | tf_op jit(solution)/shard_map/all_to_all | solution.py:79
  21.6 99.4 %all-reduce.5.cloned.1.call-start = ((), (), s32[]{:S(2)}) async-start(), calls=%async_computation.1 | async-start | bytes 1048576
  33.5 237.3 %all-reduce.7.cloned.1.call-start = ((), (), s32[]{:S(2)}) async-start(), calls=%async_computation.2 | async-start | bytes 1048576
  123.3 147.5 %copy-start.2 = (bf16[1,8192]{1,0:T(2,128)(2,1)}, bf16[1,8192]{1,0:T(2,128)(2,1)S(1)}, u32[]{:S(2)}) copy-start(bf16[1,8192]{1,0:T(2,128)(2,1)S(1)} %get-tuple-element.3) | copy-start | bytes 49156
  147.2 125.9 %copy-start.1 = (bf16[1,8192]{1,0:T(2,128)(2,1)S(1)}, bf16[1,8192]{1,0:T(2,128)(2,1)}, u32[]{:S(2)}) copy-start(bf16[1,8192]{1,0:T(2,128)(2,1)} %param.15) | copy-start | bytes 49156
Sparse Core Ops, SparseCore 0:
  33.7 87.2 all-reduce.4
  183.4 87.3 all-reduce.6
where the time goes:
time: 281 us; the launch traced here: 280 us
  waiting for transfers between devices  178 us (63%)
  matrix products  43.9 us (16%)
  blocking collectives  22.3 us (8%)
  between operations  15.5 us (6%)
  other arithmetic  7.88 us (3%)
  starting transfers between devices  7.47 us (3%)
  local copies, waits for them, and re-layouts  4.69 us (2%)
    unnamed x4, waiting for transfers between devices  172 us
    dot_general x1, matrix products, shards(): jnp.dot(picked, down_weight, preferred_element_type=jnp.float32)  23.3 us
    all_gather x1, blocking collectives, shards(): inputs = lax.all_gather(ffn_input, 'dev', axis=0, tiled=True)  22.3 us
    dot_general x1, matrix products, shards(): lax.dot_general(inputs, gate_weight, contract, preferred_element_type=jnp...  12.8 us
    all_to_all x1, starting transfers between devices, shards(): lax.all_to_all(attended, 'dev', split_axis=1, concat_axis=0, tiled=True)  7.39 us
    all_to_all x1, waiting for transfers between devices, shards(): lax.all_to_all(attended, 'dev', split_axis=1, concat_axis=0, tiled=True)  6.42 us
  transfers between devices with their start and end apart: 3, of which 3 were waited for; matrix products, arithmetic and copies ran while one was open for 1% of the time, Pallas kernels for 0%

commit v1 on v0

--- a/solution.py
+++ b/solution.py
@@ -1,13 +1,21 @@
+import functools
 import math
 
 import jax
 import jax.numpy as jnp
 from jax import lax
+from jax.experimental import pallas as pl
+from jax.experimental.pallas import tpu as pltpu
 from jax.sharding import PartitionSpec as P
 
 H = 64
 KVH = 4
 BLK = 128
+LANES = 128
+CHUNK = 256
+MAX_SLOTS = 14
+PARTS_OUT = 2
+PARTS_DOWN = 4
 
 
 def attend_rows(queries, fresh_keys, fresh_values, key_cache, value_cache, lengths):
@@ -108,6 +116,426 @@
     return (post_attention, layer_out)
 
 
+def exchange(n, me, source, target, landing, send_sem, recv_sem):
+    def copy(step, where):
+        return pltpu.make_async_remote_copy(
+            src_ref=source(lax.rem(me + step, n)),
+            dst_ref=where,
+            send_sem=send_sem.at[step],
+            recv_sem=recv_sem.at[step],
+            device_id={"dev": lax.rem(me + step, n)},
+            device_id_type=pl.DeviceIdType.MESH,
+        )
+
+    @pl.loop(1, n)
+    def _(step):
+        copy(step, target).start()
+
+    def arrived(step):
+        copy(step, landing(lax.rem(me + n - step, n))).wait_recv()
+
+    def sent():
+        @pl.loop(1, n)
+        def _(step):
+            copy(step, target).wait_send()
+
+    return arrived, sent
+
+
+def layer_kernel(
+    n,
+    residual,
+    queries,
+    fresh_keys,
+    fresh_values,
+    key_cache,
+    value_cache,
+    lengths,
+    keep_inputs,
+    keep_hidden,
+    gain,
+    out_weight,
+    gate_weight,
+    up_weight,
+    down_weight,
+    post_out,
+    layer_out,
+    keys,
+    values,
+    weights,
+    stream,
+    query_rows,
+    feature_send,
+    feature_recv,
+    row_sums,
+    own,
+    out_send,
+    out_recv,
+    down_send,
+    down_recv,
+    gathered,
+    inputs,
+    activated,
+    unit_keep,
+    cache_sem,
+    weight_sem,
+    feature_ss,
+    feature_rs,
+    out_ss,
+    out_rs,
+    gather_ss,
+    gather_rs,
+    down_ss,
+    down_rs,
+):
+    me = lax.axis_index("dev")
+    width = residual.shape[1]
+    pieces = width // LANES
+    head_dim = LANES
+    group_size = H // KVH
+    heads_here = H // n
+    cache_span = key_cache.shape[1]
+    hidden = gate_weight.shape[0]
+    starts = list(range(0, hidden, CHUNK))
+    sizes = [min(CHUNK, hidden - at) for at in starts]
+    count = len(starts)
+    out_rows = out_weight.shape[0]
+    out_count = out_rows // CHUNK
+    bf16, f32 = jnp.bfloat16, jnp.float32
+
+    barrier = pltpu.get_barrier_semaphore()
+
+    @pl.loop(1, n)
+    def _(step):
+        pl.semaphore_signal(
+            barrier,
+            inc=1,
+            device_id={"dev": lax.rem(me + step, n)},
+            device_id_type=pl.DeviceIdType.MESH,
+        )
+
+    def fetch(array, at, size, slot, sem):
+        return pltpu.make_async_copy(
+            array.at[pl.ds(at, size)], weights.at[slot, pl.ds(0, size)], weight_sem.at[sem]
+        )
+
+    key_copy = pltpu.make_async_copy(key_cache.at[0], keys, cache_sem.at[0])
+    value_copy = pltpu.make_async_copy(value_cache.at[0], values, cache_sem.at[1])
+    key_copy.start()
+    value_copy.start()
+    out_first = 2 * (count - 1)
+    out_copies = [
+        fetch(out_weight, i * CHUNK, CHUNK, out_first + i, i) for i in range(out_count)
+    ]
+    gate_copies, up_copies, down_copies = [], [], []
+    for i in range(count):
+        sem = out_count + 3 * i
+        gate_copies.append(fetch(gate_weight, starts[i], sizes[i], 2 * i, sem))
+        up_copies.append(fetch(up_weight, starts[i], sizes[i], 2 * i + 1, sem + 1))
+        down_copies.append(fetch(down_weight, starts[i], sizes[i], i, sem + 2))
+    for copy in out_copies:
+        copy.start()
+    for i in range(count - 1):
+        gate_copies[i].start()
+        up_copies[i].start()
+
+    query_row = queries[...].astype(f32)
+    residual_row = residual[...].astype(f32)
+    for c in range(pieces):
+        lanes = slice(c * LANES, (c + 1) * LANES)
+        query_rows[c : c + 1, :] = query_row[:, lanes]
+        stream[c : c + 1, :] = residual_row[:, lanes]
+
+    key_copy.wait()
+    value_copy.wait()
+    scale = 1.0 / math.sqrt(head_dim)
+    alive = lax.broadcasted_iota(jnp.int32, (group_size, cache_span), 1) < lengths[0]
+    by_lane = (((1,), (1,)), ((), ()))
+    for k in range(KVH):
+        lanes = slice(k * head_dim, (k + 1) * head_dim)
+        query = query_rows[k * group_size : (k + 1) * group_size, :]
+        scores = (
+            lax.dot_general(
+                query.astype(bf16), keys[:, lanes], by_lane, preferred_element_type=f32
+            )
+            * scale
+        )
+        scores = jnp.where(alive, scores, -1e30)
+        fresh = (
+            jnp.sum(query * fresh_keys[:, lanes].astype(f32), axis=1, keepdims=True) * scale
+        )
+        highest = jnp.maximum(jnp.max(scores, axis=1, keepdims=True), fresh)
+        cached_weights = jnp.where(alive, jnp.exp(scores - highest), 0.0)
+        fresh_weights = jnp.exp(fresh - highest)
+        totals = jnp.sum(cached_weights, axis=1, keepdims=True) + fresh_weights
+        probs = (cached_weights / totals).astype(bf16)
+        fresh_probs = (fresh_weights / totals).astype(bf16).astype(f32)
+        blended = jnp.dot(probs, values[:, lanes], preferred_element_type=f32)
+        blended = blended + fresh_probs * fresh_values[:, lanes].astype(f32)
+        blended = blended.astype(bf16).astype(f32)
+        for at in range(0, group_size, heads_here):
+            feature_send[(k * group_size + at) // heads_here] = blended[at : at + heads_here]
+
+    pl.semaphore_wait(barrier, n - 1)
+    arrived, features_sent = exchange(
+        n,
+        me,
+        lambda peer: feature_send.at[peer],
+        feature_recv.at[me],
+        lambda peer: feature_recv.at[peer],
+        feature_ss,
+        feature_rs,
+    )
+    feature_recv[pl.ds(me, 1)] = feature_send[pl.ds(me, 1)]
+
+    blocks = keep_hidden.shape[1]
+    unit = me * hidden + lax.broadcasted_iota(jnp.int32, (blocks, hidden), 1)
+    first = BLK * lax.broadcasted_iota(jnp.int32, (blocks, hidden), 0)
+    selector = jnp.where((unit >= first) & (unit < first + BLK), 1.0, 0.0).astype(bf16)
+    unit_keep[...] = jnp.dot(
+        keep_hidden[...].astype(f32).astype(bf16), selector, preferred_element_type=f32
+    )
+
+    for copy in out_copies:
+        copy.wait()
+
+    @pl.loop(1, n)
+    def _(step):
+        arrived(step)
+
+    def send_sums(part, parts, product, send, recv, send_sem, recv_sem):
+        rows = pieces // parts
+        for c in range(rows):
+            row_sums[:, part * rows + c, :] = product[:, c * LANES : (c + 1) * LANES]
+        here = pl.ds(part * rows, rows)
+
+        @pl.loop(0, n)
+        def _(r):
+            send[part, r] = row_sums[r, here].astype(bf16)
+
+        started = exchange(
+            n,
+            me,
+            lambda peer: send.at[part, peer],
+            recv.at[part, me],
+            lambda peer: recv.at[part, peer],
+            send_sem.at[part],
+            recv_sem.at[part],
+        )
+        own[here] = row_sums[me, here]
+        return started
+
+    def add_sums(part, parts, started, recv):
+        rows = pieces // parts
+        here = pl.ds(part * rows, rows)
+
+        def add(step, total):
+            started[0](step)
+            return total + recv[part, lax.rem(me + n - step, n)].astype(f32)
+
+        total = lax.fori_loop(1, n, add, own[here])
+        return total
+
+    features = jnp.concatenate(
+        [feature_recv[:, h, :].astype(bf16) for h in range(heads_here)], axis=1
+    )
+    out_started = []
+    part_width = width // PARTS_OUT
+    for part in range(PARTS_OUT):
+        columns = slice(part * part_width, (part + 1) * part_width)
+        product = None
+        for i in range(out_count):
+            term = jnp.dot(
+                features[:, i * CHUNK : (i + 1) * CHUNK],
+                weights[out_first + i, :, columns],
+                preferred_element_type=f32,
+            )
+            product = term if product is None else product + term
+        out_started.append(
+            send_sums(part, PARTS_OUT, product, out_send, out_recv, out_ss, out_rs)
+        )
+    gate_copies[count - 1].start()
+    up_copies[count - 1].start()
+    for part in range(PARTS_OUT):
+        rows = pieces // PARTS_OUT
+        here = pl.ds(part * rows, rows)
+        total = add_sums(part, PARTS_OUT, out_started[part], out_recv)
+        stream[here] = (stream[here] + total).astype(bf16).astype(f32)
+
+    post = stream[...]
+    squares = jnp.sum(jnp.sum(post * post, axis=1, keepdims=True), axis=0, keepdims=True) / width
+    mask_row = jnp.broadcast_to(keep_inputs[pl.ds(me, 1), :].astype(f32), (pieces, pieces))
+    diagonal = lax.broadcasted_iota(jnp.int32, (pieces, pieces), 0) == lax.broadcasted_iota(
+        jnp.int32, (pieces, pieces), 1
+    )
+    mask = jnp.sum(jnp.where(diagonal, mask_row, 0.0), axis=1, keepdims=True)
+    scaled = post * lax.rsqrt(squares + 1e-05) * gain[...] * mask
+    gathered[me] = scaled.astype(bf16)
+    arrived, inputs_sent = exchange(
+        n,
+        me,
+        lambda peer: gathered.at[me],
+        gathered.at[me],
+        lambda peer: gathered.at[peer],
+        gather_ss,
+        gather_rs,
+    )
+    for c in range(pieces):
+        post_out[:, c * LANES : (c + 1) * LANES] = stream[c : c + 1, :].astype(bf16)
+    row_sums[me] = scaled.astype(bf16).astype(f32)
+
+    @pl.loop(1, n)
+    def _(step):
+        arrived(step)
+        peer = lax.rem(me + n - step, n)
+        row_sums[peer] = gathered[peer].astype(f32)
+
+    for c in range(pieces):
+        inputs[:, c * LANES : (c + 1) * LANES] = row_sums[:, c, :].astype(bf16)
+
+    for i in range(count):
+        gate_copies[i].wait()
+        up_copies[i].wait()
+        units = slice(starts[i], starts[i] + sizes[i])
+        gate = lax.dot_general(
+            inputs[...], weights[2 * i, 0 : sizes[i], :], by_lane, preferred_element_type=f32
+        )
+        up = lax.dot_general(
+            inputs[...], weights[2 * i + 1, 0 : sizes[i], :], by_lane, preferred_element_type=f32
+        )
+        silu = gate / (1.0 + jnp.exp(-gate))
+        activated[:, units] = (silu * up * unit_keep[:, units]).astype(bf16)
+        for j in (2 * i, 2 * i + 1):
+            if j < count:
+                down_copies[j].start()
+
+    for copy in down_copies:
+        copy.wait()
+    down_started = []
+    part_width = width // PARTS_DOWN
+    for part in range(PARTS_DOWN):
+        columns = slice(part * part_width, (part + 1) * part_width)
+        product = None
+        for i in range(count):
+            term = jnp.dot(
+                activated[:, starts[i] : starts[i] + sizes[i]],
+                weights[i, 0 : sizes[i], columns],
+                preferred_element_type=f32,
+            )
+            product = term if product is None else product + term
+        down_started.append(
+            send_sums(part, PARTS_DOWN, product, down_send, down_recv, down_ss, down_rs)
+        )
+    for part in range(PARTS_DOWN):
+        rows = pieces // PARTS_DOWN
+        here = pl.ds(part * rows, rows)
+        total = add_sums(part, PARTS_DOWN, down_started[part], down_recv)
+        stream[here] = stream[here] + total
+    for c in range(pieces):
+        layer_out[:, c * LANES : (c + 1) * LANES] = stream[c : c + 1, :].astype(bf16)
+
+    features_sent()
+    inputs_sent()
+    for started in out_started + down_started:
+        started[1]()
+
+
+def fused_layer(n, *operands):
+    (
+        residual,
+        _,
+        _,
+        _,
+        key_cache,
+        _,
+        _,
+        keep_inputs,
+        keep_hidden,
+        norm_gain,
+        out_weight,
+        gate_weight,
+        _,
+        _,
+    ) = operands
+    width = residual.shape[1]
+    pieces = width // LANES
+    hidden = gate_weight.shape[0]
+    count = -(-hidden // CHUNK)
+    slots = 2 * count
+    bf16, f32 = jnp.bfloat16, jnp.float32
+    dma = pltpu.SemaphoreType.DMA
+    vmem = pl.BlockSpec(memory_space=pltpu.VMEM)
+    smem = pl.BlockSpec(memory_space=pltpu.SMEM)
+    hbm = pl.BlockSpec(memory_space=pl.ANY)
+    operands = list(operands)
+    operands[9] = norm_gain.reshape(pieces, LANES)
+    cache_shape = key_cache.shape[1:]
+    row_shape = jax.ShapeDtypeStruct(residual.shape, bf16)
+    weight_bytes = 2 * (out_weight.size + 3 * gate_weight.size)
+    return pl.pallas_call(
+        functools.partial(layer_kernel, n),
+        out_shape=(row_shape, row_shape),
+        in_specs=[vmem] * 4 + [hbm] * 2 + [smem] + [vmem] * 3 + [hbm] * 4,
+        out_specs=(vmem, vmem),
+        scratch_shapes=[
+            pltpu.VMEM(cache_shape, bf16),
+            pltpu.VMEM(cache_shape, bf16),
+            pltpu.VMEM((slots, CHUNK, width), bf16),
+            pltpu.VMEM((pieces, LANES), f32),
+            pltpu.VMEM((pieces, LANES), f32),
+            pltpu.VMEM((n, H // n, LANES), f32),
+            pltpu.VMEM((n, H // n, LANES), f32),
+            pltpu.VMEM((n, pieces, LANES), f32),
+            pltpu.VMEM((pieces, LANES), f32),
+            pltpu.VMEM((PARTS_OUT, n, pieces // PARTS_OUT, LANES), bf16),
+            pltpu.VMEM((PARTS_OUT, n, pieces // PARTS_OUT, LANES), bf16),
+            pltpu.VMEM((PARTS_DOWN, n, pieces // PARTS_DOWN, LANES), bf16),
+            pltpu.VMEM((PARTS_DOWN, n, pieces // PARTS_DOWN, LANES), bf16),
+            pltpu.VMEM((n, pieces, LANES), bf16),
+            pltpu.VMEM((n, width), bf16),
+            pltpu.VMEM((n, hidden), bf16),
+            pltpu.VMEM((n, hidden), f32),
+            dma((2,)),
+            dma((out_weight.shape[0] // CHUNK + 3 * count,)),
+            dma((n,)),
+            dma((n,)),
+            dma((PARTS_OUT, n)),
+            dma((PARTS_OUT, n)),
+            dma((n,)),
+            dma((n,)),
+            dma((PARTS_DOWN, n)),
+            dma((PARTS_DOWN, n)),
+        ],
+        compiler_params=pltpu.CompilerParams(
+            collective_id=0, has_side_effects=True, vmem_limit_bytes=63 * 2**20
+        ),
+        cost_estimate=pl.CostEstimate(
+            flops=n * weight_bytes, bytes_accessed=weight_bytes, transcendentals=0
+        ),
+        name="layer",
+    )(*operands)
+
+
+def one_row_each(n, *operands):
+    residual, gate_weight, out_weight = operands[0], operands[11], operands[10]
+    slots = 2 * -(-gate_weight.shape[0] // CHUNK)
+    return (
+        residual.shape[0] == 1
+        and n % 16 == 0
+        and (H // KVH) % max(H // n, 1) == 0
+        and out_weight.shape[0] == (H // n) * LANES
+        and out_weight.shape[0] == 2 * CHUNK
+        and 2 < slots <= MAX_SLOTS
+        and gate_weight.shape[0] % 64 == 0
+    )
+
+
+def layer(n, *operands):
+    if one_row_each(n, *operands):
+        return fused_layer(n, *operands)
+    return shards(*operands)
+
+
 def solution(mesh):
     in_specs = (
         P(("group", "dev"), None),
@@ -126,4 +554,5 @@
         P("dev", None),
     )
     out_specs = (P(("group", "dev"), None), P(("group", "dev"), None))
-    return jax.shard_map(shards, mesh=mesh, in_specs=in_specs, out_specs=out_specs, check_vma=False)
+    body = functools.partial(layer, mesh.shape["dev"])
+    return jax.shard_map(body, mesh=mesh, in_specs=in_specs, out_specs=out_specs, check_vma=False)

time: 281 us -> 76.6 us (0.27)
  waiting for transfers between devices: 178 us -> 0 us
  Pallas kernels: 0 us -> 72.2 us
  matrix products: 43.9 us -> 0 us
  blocking collectives: 22.3 us -> 0 us
  between operations: 15.5 us -> 1.29 us
  other arithmetic: 7.88 us -> 0 us
  starting transfers between devices: 7.47 us -> 0 us
    unnamed x4 -> x0, waiting for transfers between devices: 172 us -> none
    pallas_call x0 -> x1, Pallas kernels: none -> 72.2 us  [fused_layer(): pl.pallas_call(functools.partial(layer_kernel, n), out_shape=(row_shape,...]
    dot_general x7 -> x0, matrix products: 43.9 us -> none  [the longest x1 23.3 us: shards(): jnp.dot(picked, down_weight, preferred_element_type=jnp.float32)]
    all_gather x1 -> x0, blocking collectives: 22.3 us -> none  [shards(): inputs = lax.all_gather(ffn_input, 'dev', axis=0, tiled=True)]
    all_to_all x1 -> x0, starting transfers between devices: 7.39 us -> none  [shards(): lax.all_to_all(attended, 'dev', split_axis=1, concat_axis=0, tiled=True)]
    all_to_all x1 -> x0, waiting for transfers between devices: 6.42 us -> none  [shards(): lax.all_to_all(attended, 'dev', split_axis=1, concat_axis=0, tiled=True)]
    convert_element_type x4 -> x0, other arithmetic: 3.7 us -> none  [the longest x1 2.3 us: shards(): (post_attention.astype(jnp.float32) + ffn_out).astype(jnp.bfloat16)]
  transfers between devices with their start and end apart: 3 -> 0, of which waited for: 3 -> 0; matrix products, arithmetic and copies ran while one was open for 1% -> 0% of each run, Pallas kernels for 0% -> 0%
where the time goes in v1:
time: 76.6 us; the launch traced here: 76.3 us
  Pallas kernels  72.2 us (94%)
  local copies, waits for them, and re-layouts  2.81 us (4%)
  between operations  1.29 us (2%)
    pallas_call x1, Pallas kernels, fused_layer(): pl.pallas_call(functools.partial(layer_kernel, n), out_shape=(row_shape,...  72.2 us
    unnamed x2, local copies, waits for them, and re-layouts  2.81 us

profile of v1, /device:TPU:0, one launch (start us, length us, event | category | flops | bytes accessed | tf_op | source)
XLA Modules:
  0.0 76.3 jit_solution(6473610084515524684)
XLA Ops:
  1.3 72.2 %layer.1 = (bf16[1,8192]{1,0:T(2,128)(2,1)}, bf16[1,8192]{1,0:T(2,128)(2,1)}) custom-call(bf16[1,8192]{1,0:T(2,128)(2,1)} %residual.1, bf16[1,8192]{1,0:T(2,128)(2,1)} %queries.1, bf16[1,512]{1,0:T(2,128)(2,1)} %fresh_keys.1, bf16[1,512]{1,0:T(2,128)(2,1)} %fresh_values.1, bf16[1,320,512]{2,1,0:T(8,128)(2,1)} %key_cache.1, bf16[1,320,512]{2,1,0:T(8,128)(2,1)} %value_cache.1, ...), custom_call_target="tpu_custom_call" | custom-call | flops 1493172224 | bytes 93323264 | tf_op jit(solution)/shard_map/layer/pallas_call | solution.py:475
  73.4 1.4 %copy.19 = bf16[1,8192]{1,0:T(2,128)(2,1)} copy(bf16[1,8192]{1,0:T(2,128)(2,1)} %get-tuple-element.4) | data formatting | bytes 32768
  74.8 1.4 %copy.20 = bf16[1,8192]{1,0:T(2,128)(2,1)} copy(bf16[1,8192]{1,0:T(2,128)(2,1)} %get-tuple-element.5) | data formatting | bytes 32768

commit v2 on v1

--- a/solution.py
+++ b/solution.py
@@ -116,26 +116,26 @@
     return (post_attention, layer_out)
 
 
-def exchange(n, me, source, target, landing, send_sem, recv_sem):
+def exchange(count, to, source, target, landing, send_sem, recv_sem):
     def copy(step, where):
         return pltpu.make_async_remote_copy(
-            src_ref=source(lax.rem(me + step, n)),
+            src_ref=source(step),
             dst_ref=where,
             send_sem=send_sem.at[step],
             recv_sem=recv_sem.at[step],
-            device_id={"dev": lax.rem(me + step, n)},
+            device_id={"dev": to(step)},
             device_id_type=pl.DeviceIdType.MESH,
         )
 
-    @pl.loop(1, n)
+    @pl.loop(1, count)
     def _(step):
         copy(step, target).start()
 
     def arrived(step):
-        copy(step, landing(lax.rem(me + n - step, n))).wait_recv()
+        copy(step, landing(step)).wait_recv()
 
     def sent():
-        @pl.loop(1, n)
+        @pl.loop(1, count)
         def _(step):
             copy(step, target).wait_send()
 
@@ -169,10 +169,10 @@
     feature_recv,
     row_sums,
     own,
-    out_send,
-    out_recv,
-    down_send,
-    down_recv,
+    out_near,
+    out_far,
+    down_near,
+    down_far,
     gathered,
     inputs,
     activated,
@@ -185,10 +185,22 @@
     out_rs,
     gather_ss,
     gather_rs,
+    relay_ss,
+    relay_rs,
     down_ss,
     down_rs,
 ):
     me = lax.axis_index("dev")
+    pairs = n // 2
+    pair, side = me // 2, lax.rem(me, 2)
+    partner = me + 1 - 2 * side
+
+    def pair_to(step):
+        return lax.rem(pair + step, pairs)
+
+    def pair_from(step):
+        return lax.rem(pair + pairs - step, pairs)
+
     width = residual.shape[1]
     pieces = width // LANES
     head_dim = LANES
@@ -236,8 +248,8 @@
     for copy in out_copies:
         copy.start()
     for i in range(count - 1):
-        gate_copies[i].start()
-        up_copies[i].start()
+        gate_copies[i].start(priority=1)
+        up_copies[i].start(priority=1)
 
     query_row = queries[...].astype(f32)
     residual_row = residual[...].astype(f32)
@@ -279,10 +291,10 @@
     pl.semaphore_wait(barrier, n - 1)
     arrived, features_sent = exchange(
         n,
-        me,
-        lambda peer: feature_send.at[peer],
+        lambda step: lax.rem(me + step, n),
+        lambda step: feature_send.at[lax.rem(me + step, n)],
         feature_recv.at[me],
-        lambda peer: feature_recv.at[peer],
+        lambda step: feature_recv.at[lax.rem(me + n - step, n)],
         feature_ss,
         feature_rs,
     )
@@ -303,43 +315,65 @@
     def _(step):
         arrived(step)
 
-    def send_sums(part, parts, product, send, recv, send_sem, recv_sem):
+    def pair_copy(part, near, sems):
+        return pltpu.make_async_remote_copy(
+            src_ref=near.at[0, part],
+            dst_ref=near.at[1, part],
+            send_sem=sems[0].at[part, 0],
+            recv_sem=sems[1].at[part, 0],
+            device_id={"dev": partner},
+            device_id_type=pl.DeviceIdType.MESH,
+        )
+
+    def to_partner(part, parts, product, near, sems):
         rows = pieces // parts
+        here = pl.ds(part * rows, rows)
         for c in range(rows):
             row_sums[:, part * rows + c, :] = product[:, c * LANES : (c + 1) * LANES]
-        here = pl.ds(part * rows, rows)
-
-        @pl.loop(0, n)
+
+        @pl.loop(0, pairs)
         def _(r):
-            send[part, r] = row_sums[r, here].astype(bf16)
-
-        started = exchange(
-            n,
-            me,
-            lambda peer: send.at[part, peer],
-            recv.at[part, me],
-            lambda peer: recv.at[part, peer],
-            send_sem.at[part],
-            recv_sem.at[part],
-        )
-        own[here] = row_sums[me, here]
-        return started
-
-    def add_sums(part, parts, started, recv):
+            near[0, part, r] = row_sums[2 * r + 1 - side, here].astype(bf16)
+
+        pair_copy(part, near, sems).start()
+
+    def to_owners(part, parts, near, far, sems):
         rows = pieces // parts
         here = pl.ds(part * rows, rows)
+        pair_copy(part, near, sems).wait_recv()
+
+        @pl.loop(0, pairs)
+        def _(r):
+            both = row_sums[2 * r + side, here] + near[1, part, r].astype(f32)
+            far[0, part, r] = both.astype(bf16)
+
+        started = exchange(
+            pairs,
+            lambda step: 2 * pair_to(step) + side,
+            lambda step: far.at[0, part, pair_to(step)],
+            far.at[1, part, pair],
+            lambda step: far.at[1, part, pair_from(step)],
+            sems[0].at[part],
+            sems[1].at[part],
+        )
+        own[here] = row_sums[me, here] + near[1, part, pair].astype(f32)
+        return started
+
+    def add_sums(part, parts, started, far):
+        rows = pieces // parts
+        here = pl.ds(part * rows, rows)
 
         def add(step, total):
             started[0](step)
-            return total + recv[part, lax.rem(me + n - step, n)].astype(f32)
-
-        total = lax.fori_loop(1, n, add, own[here])
-        return total
+            return total + far[1, part, pair_from(step)].astype(f32)
+
+        return lax.fori_loop(1, pairs, add, own[here])
 
     features = jnp.concatenate(
         [feature_recv[:, h, :].astype(bf16) for h in range(heads_here)], axis=1
     )
     out_started = []
+    out_sems, down_sems = (out_ss, out_rs), (down_ss, down_rs)
     part_width = width // PARTS_OUT
     for part in range(PARTS_OUT):
         columns = slice(part * part_width, (part + 1) * part_width)
@@ -351,15 +385,15 @@
                 preferred_element_type=f32,
             )
             product = term if product is None else product + term
-        out_started.append(
-            send_sums(part, PARTS_OUT, product, out_send, out_recv, out_ss, out_rs)
-        )
-    gate_copies[count - 1].start()
-    up_copies[count - 1].start()
+        to_partner(part, PARTS_OUT, product, out_near, out_sems)
+    gate_copies[count - 1].start(priority=1)
+    up_copies[count - 1].start(priority=1)
+    for part in range(PARTS_OUT):
+        out_started.append(to_owners(part, PARTS_OUT, out_near, out_far, out_sems))
     for part in range(PARTS_OUT):
         rows = pieces // PARTS_OUT
         here = pl.ds(part * rows, rows)
-        total = add_sums(part, PARTS_OUT, out_started[part], out_recv)
+        total = add_sums(part, PARTS_OUT, out_started[part], out_far)
         stream[here] = (stream[here] + total).astype(bf16).astype(f32)
 
     post = stream[...]
@@ -372,23 +406,42 @@
     scaled = post * lax.rsqrt(squares + 1e-05) * gain[...] * mask
     gathered[me] = scaled.astype(bf16)
     arrived, inputs_sent = exchange(
-        n,
-        me,
-        lambda peer: gathered.at[me],
+        pairs,
+        lambda step: 2 * pair_to(step) + side,
+        lambda step: gathered.at[me],
         gathered.at[me],
-        lambda peer: gathered.at[peer],
+        lambda step: gathered.at[2 * pair_from(step) + side],
         gather_ss,
         gather_rs,
     )
+
+    def relay(step, row):
+        return pltpu.make_async_remote_copy(
+            src_ref=gathered.at[2 * pair_from(step) + side],
+            dst_ref=gathered.at[row],
+            send_sem=relay_ss.at[step],
+            recv_sem=relay_rs.at[step],
+            device_id={"dev": partner},
+            device_id_type=pl.DeviceIdType.MESH,
+        )
+
+    relay(0, me).start()
     for c in range(pieces):
         post_out[:, c * LANES : (c + 1) * LANES] = stream[c : c + 1, :].astype(bf16)
     row_sums[me] = scaled.astype(bf16).astype(f32)
 
-    @pl.loop(1, n)
+    @pl.loop(1, pairs)
     def _(step):
         arrived(step)
-        peer = lax.rem(me + n - step, n)
-        row_sums[peer] = gathered[peer].astype(f32)
+        row = 2 * pair_from(step) + side
+        relay(step, row).start()
+        row_sums[row] = gathered[row].astype(f32)
+
+    @pl.loop(0, pairs)
+    def _(step):
+        row = 2 * pair_from(step) + 1 - side
+        relay(step, row).wait_recv()
+        row_sums[row] = gathered[row].astype(f32)
 
     for c in range(pieces):
         inputs[:, c * LANES : (c + 1) * LANES] = row_sums[:, c, :].astype(bf16)
@@ -407,7 +460,7 @@
         activated[:, units] = (silu * up * unit_keep[:, units]).astype(bf16)
         for j in (2 * i, 2 * i + 1):
             if j < count:
-                down_copies[j].start()
+                down_copies[j].start(priority=1)
 
     for copy in down_copies:
         copy.wait()
@@ -423,13 +476,14 @@
                 preferred_element_type=f32,
             )
             product = term if product is None else product + term
-        down_started.append(
-            send_sums(part, PARTS_DOWN, product, down_send, down_recv, down_ss, down_rs)
-        )
+        to_partner(part, PARTS_DOWN, product, down_near, down_sems)
+        if part > 0:
+            down_started.append(to_owners(part - 1, PARTS_DOWN, down_near, down_far, down_sems))
+    down_started.append(to_owners(PARTS_DOWN - 1, PARTS_DOWN, down_near, down_far, down_sems))
     for part in range(PARTS_DOWN):
         rows = pieces // PARTS_DOWN
         here = pl.ds(part * rows, rows)
-        total = add_sums(part, PARTS_DOWN, down_started[part], down_recv)
+        total = add_sums(part, PARTS_DOWN, down_started[part], down_far)
         stream[here] = stream[here] + total
     for c in range(pieces):
         layer_out[:, c * LANES : (c + 1) * LANES] = stream[c : c + 1, :].astype(bf16)
@@ -438,6 +492,14 @@
     inputs_sent()
     for started in out_started + down_started:
         started[1]()
+    for part in range(PARTS_OUT):
+        pair_copy(part, out_near, out_sems).wait_send()
+    for part in range(PARTS_DOWN):
+        pair_copy(part, down_near, down_sems).wait_send()
+
+    @pl.loop(0, pairs)
+    def _(step):
+        relay(step, me).wait_send()
 
 
 def fused_layer(n, *operands):
@@ -487,10 +549,10 @@
             pltpu.VMEM((n, H // n, LANES), f32),
             pltpu.VMEM((n, pieces, LANES), f32),
             pltpu.VMEM((pieces, LANES), f32),
-            pltpu.VMEM((PARTS_OUT, n, pieces // PARTS_OUT, LANES), bf16),
-            pltpu.VMEM((PARTS_OUT, n, pieces // PARTS_OUT, LANES), bf16),
-            pltpu.VMEM((PARTS_DOWN, n, pieces // PARTS_DOWN, LANES), bf16),
-            pltpu.VMEM((PARTS_DOWN, n, pieces // PARTS_DOWN, LANES), bf16),
+            pltpu.VMEM((2, PARTS_OUT, n // 2, pieces // PARTS_OUT, LANES), bf16),
+            pltpu.VMEM((2, PARTS_OUT, n // 2, pieces // PARTS_OUT, LANES), bf16),
+            pltpu.VMEM((2, PARTS_DOWN, n // 2, pieces // PARTS_DOWN, LANES), bf16),
+            pltpu.VMEM((2, PARTS_DOWN, n // 2, pieces // PARTS_DOWN, LANES), bf16),
             pltpu.VMEM((n, pieces, LANES), bf16),
             pltpu.VMEM((n, width), bf16),
             pltpu.VMEM((n, hidden), bf16),
@@ -499,12 +561,14 @@
             dma((out_weight.shape[0] // CHUNK + 3 * count,)),
             dma((n,)),
             dma((n,)),
-            dma((PARTS_OUT, n)),
-            dma((PARTS_OUT, n)),
-            dma((n,)),
-            dma((n,)),
-            dma((PARTS_DOWN, n)),
-            dma((PARTS_DOWN, n)),
+            dma((PARTS_OUT, n // 2)),
+            dma((PARTS_OUT, n // 2)),
+            dma((n // 2,)),
+            dma((n // 2,)),
+            dma((n // 2,)),
+            dma((n // 2,)),
+            dma((PARTS_DOWN, n // 2)),
+            dma((PARTS_DOWN, n // 2)),
         ],
         compiler_params=pltpu.CompilerParams(
             collective_id=0, has_side_effects=True, vmem_limit_bytes=63 * 2**20

time: 76.6 us -> 59.3 us (0.77)
  Pallas kernels: 72.2 us -> 54.9 us
    pallas_call x1, Pallas kernels: 72.2 us -> 54.9 us  [fused_layer(): pl.pallas_call(functools.partial(layer_kernel, n), out_shape=(row_shape,...]
where the time goes in v2:
time: 59.3 us; the launch traced here: 59 us
  Pallas kernels  54.9 us (93%)
  local copies, waits for them, and re-layouts  2.81 us (5%)
  between operations  1.29 us (2%)
    pallas_call x1, Pallas kernels, fused_layer(): pl.pallas_call(functools.partial(layer_kernel, n), out_shape=(row_shape,...  54.9 us
    unnamed x2, local copies, waits for them, and re-layouts  2.81 us

profile of v2, /device:TPU:0, one launch (start us, length us, event | category | flops | bytes accessed | tf_op | source)
XLA Modules:
  0.0 59.0 jit_solution(6792903513528618283)
XLA Ops:
  1.3 54.9 %layer.1 = (bf16[1,8192]{1,0:T(2,128)(2,1)}, bf16[1,8192]{1,0:T(2,128)(2,1)}) custom-call(bf16[1,8192]{1,0:T(2,128)(2,1)} %residual.1, bf16[1,8192]{1,0:T(2,128)(2,1)} %queries.1, bf16[1,512]{1,0:T(2,128)(2,1)} %fresh_keys.1, bf16[1,512]{1,0:T(2,128)(2,1)} %fresh_values.1, bf16[1,320,512]{2,1,0:T(8,128)(2,1)} %key_cache.1, bf16[1,320,512]{2,1,0:T(8,128)(2,1)} %value_cache.1, ...), custom_call_target="tpu_custom_call" | custom-call | flops 1493172224 | bytes 93323264 | tf_op jit(solution)/shard_map/layer/pallas_call | solution.py:537
  56.1 1.4 %copy.19 = bf16[1,8192]{1,0:T(2,128)(2,1)} copy(bf16[1,8192]{1,0:T(2,128)(2,1)} %get-tuple-element.4) | data formatting | bytes 32768
  57.5 1.4 %copy.20 = bf16[1,8192]{1,0:T(2,128)(2,1)} copy(bf16[1,8192]{1,0:T(2,128)(2,1)} %get-tuple-element.5) | data formatting | bytes 32768
